TPU v7x, 128 devices: a whole 4x4x4 slice. The times are simulated.
128 devices in a mesh: section: 4 (over x_hi, core), expert: 32 (over x_lo, z, y).
Axes of the slice: x: 4 (x_hi: 2, x_lo: 2; x = x_hi * 2 + x_lo), y: 4, z: 4, core: 2. Of those that a mesh axis runs over, the one named last changes fastest.
Arguments:
- batches: bfloat16 [4, 2048, 3584], P(None, 'expert'), may hold values from -6 to 6
- order: int32 [4], replicated, may hold values from 0 to 3, each once
- gains: float32 [4, 3584], P('section'), may hold values from 0.25 to 1.75
- router: float32 [4, 3584, 8], P('section'), may hold values from -0.09375 to 0.09375
- routes: int32 [4, 2, 2048, 2], P('section', None, 'expert'), may hold values from 0 to 7, all different within a row; in each aligned block of 64 rows (0 to 63, 64 to 127, ..., all dimensions but the last counted through in order) at most 18 rows name the same one
- caps: int32 [4, 8], P('section'), may hold values from 9 to 18, as said below
- w_in: bfloat16 [4, 2, 3584, 16384], P('section', None, None, 'expert'), may hold values from -0.09375 to 0.09375
- w_down: bfloat16 [4, 16384, 3584], P('section', 'expert'), may hold values from -0.125 to 0.125
Outputs:
- acts: bfloat16 [4, 2, 2048, 3584], P('section', None, 'expert')
Inputs may be any that keep to these rules, and one draw needn't show every extreme that they name: `caps`: each layer has at least one expert of capacity exactly 18. `routes`: no expert is named by more than 18 pairs among the tokens of one index of expert.
All inputs are finite; a program needn't handle non-finite values.
Results may differ from a plain program's by a relative error of at most 0.028.
Values may be sent and summed in bfloat16 or wider, within the bound.
A program may use at most 128 MiB of HBM per device.

v0:
```python
import jax
import jax.numpy as jnp
from jax import lax
from jax.sharding import PartitionSpec as P

D = 3584
EXPERTS = 8
TOPK = 2
CAP = 18


def shifted(value, axis, steps):
    count = lax.axis_size(axis)
    leading, last = (max(0, -steps), min(count, count - steps))
    return lax.ppermute(value, axis, [(source, source + steps) for source in range(leading, last)])


def run_layer(tokens_in, gain, router_w, cap_row, route_row, gate_up, down):
    tok_rows = tokens_in.shape[0]
    x32 = tokens_in.astype(jnp.float32)
    normed = (x32 * lax.rsqrt(jnp.mean(x32 * x32, axis=-1, keepdims=True) + 1e-06) * gain).astype(
        jnp.bfloat16
    )
    logits = jnp.dot(normed.astype(jnp.float32), router_w, precision=lax.Precision.HIGHEST)
    scores = jax.nn.sigmoid(logits)
    chosen = jnp.take_along_axis(scores, route_row, axis=1)
    gates = 2.5 * chosen / jnp.sum(chosen, axis=1, keepdims=True)
    flat = route_row.reshape(-1)
    onehot = (flat[:, None] == jnp.arange(EXPERTS, dtype=jnp.int32)[None, :]).astype(jnp.int32)
    ranks = jnp.sum((jnp.cumsum(onehot, axis=0) - onehot) * onehot, axis=-1)
    kept = ranks < cap_row[flat]
    slots = jnp.where(kept, flat * CAP + ranks, EXPERTS * CAP)
    select = (slots[None, :] == jnp.arange(EXPERTS * CAP, dtype=jnp.int32)[:, None]).astype(
        jnp.bfloat16
    )
    rows = jnp.repeat(normed, TOPK, axis=0)
    packed = jnp.dot(select, rows, preferred_element_type=jnp.float32).astype(jnp.bfloat16)
    devices = lax.axis_size("expert")
    pieces = devices // EXPERTS
    packed = packed.reshape(EXPERTS, 1, CAP, D)
    outgoing = jnp.broadcast_to(packed, (EXPERTS, pieces, CAP, D)).reshape(devices, CAP, D)
    arrived = lax.all_to_all(outgoing, "expert", split_axis=0, concat_axis=0, tiled=True)
    senders = arrived.shape[0]
    count = arrived.shape[1]
    flat_rows = arrived.reshape(-1, D)
    both = jnp.einsum("rd,gdf->grf", flat_rows, gate_up, preferred_element_type=jnp.float32)
    hidden = (jax.nn.silu(both[0]) * both[1]).astype(jnp.bfloat16)
    partial_out = jnp.dot(hidden, down, preferred_element_type=jnp.float32).astype(jnp.bfloat16)
    computed = partial_out.reshape(senders, count, D)
    back = lax.all_to_all(computed, "expert", split_axis=0, concat_axis=0, tiled=True)
    summed = jnp.sum(back.reshape(EXPERTS, pieces, CAP, D).astype(jnp.float32), axis=1).reshape(
        EXPERTS * CAP, D
    )
    picked = jnp.take(summed, jnp.where(kept, slots, 0), axis=0)
    weight = gates.reshape(-1) * kept.astype(jnp.float32)
    moe = jnp.sum((picked * weight[:, None]).reshape(tok_rows, TOPK, D), axis=1)
    return (x32 + moe).astype(jnp.bfloat16)


def local(batches, order, gains, router, routes, caps, w_in, w_down):
    sections = lax.axis_size("section")
    position = lax.axis_index("section")
    first_input = lax.dynamic_index_in_dim(batches, order[0], 0, keepdims=False)
    second_input = lax.dynamic_index_in_dim(batches, order[1], 0, keepdims=False)
    from_below = jnp.where(position == 0, first_input, jnp.zeros_like(first_input))
    from_above = jnp.where(position == sections - 1, second_input, jnp.zeros_like(second_input))
    results = jnp.zeros((2,) + first_input.shape, jnp.bfloat16)
    for tick in range(sections):
        going_down = position == tick
        going_up = position == sections - 1 - tick
        current = jnp.where(going_down, from_below, from_above)
        direction = jnp.where(going_down, 0, 1).astype(jnp.int32)
        route_row = lax.dynamic_index_in_dim(routes[0], direction, 0, keepdims=False)
        output = run_layer(current, gains[0], router[0], caps[0], route_row, w_in[0], w_down[0])
        output = jnp.where(going_down | going_up, output, jnp.zeros_like(output))
        results = jnp.where(going_down, results.at[0].set(output), results)
        results = jnp.where(going_up, results.at[1].set(output), results)
        if tick + 1 < sections:
            from_below = shifted(output, "section", 1)
            from_above = shifted(output, "section", -1)
    return results[None]


def solution(mesh):
    placed = (
        P(None, "expert", None),
        P(),
        P("section", None),
        P("section", None, None),
        P("section", None, "expert", None),
        P("section", None),
        P("section", None, None, "expert"),
        P("section", "expert", None),
    )
    return jax.shard_map(
        local,
        mesh=mesh,
        in_specs=placed,
        out_specs=P("section", None, "expert", None),
        check_vma=False,
    )
```

profile of v0, /device:TPU:19, one launch (start us, length us, event | category | flops | bytes accessed | tf_op | source)
XLA Modules:
  0.0 853.4 jit_solution(13206995817169524312)
XLA Ops:
  13.4 5.7 compare_and_fusion.2
  22.3 71.3 %all_to_all.40 = bf16[32,18,3584]{2,1,0:T(8,128)(2,1)} all-to-all(bf16[32,18,3584]{2,1,0:T(8,128)(2,1)S(1)} %bitcast.242), channel_id=1, replica_groups=mesh['section'=4,'expert'=32] {'expert'}, dimensions={0} | all-to-all | bytes 8257536 | tf_op jit(solution)/shard_map/all_to_all | solution.py:42
  93.7 7.3 reshape.1032
  101.0 8.1 fusion.12
  113.5 7.3 reshape.637
  120.7 6.7 all-to-all-start.1
  129.8 66.4 %all-to-all-done.1 = bf16[32,18,3584]{2,1,0:T(8,128)(2,1)} async-done(((bf16[32,18,3584]{2,1,0:T(8,128)(2,1)}), bf16[32,18,3584]{2,1,0:T(8,128)(2,1)}, u32[]{:S(2)}, u32[]{:S(2)}) %all-to-all-start.1) | async-done | bytes 4128800 | tf_op jit(solution)/shard_map/all_to_all | solution.py:50
  213.8 7.5 collective-permute-start
  226.7 5.9 collective-permute-done.1
  239.5 64.7 %all_to_all.41 = bf16[32,18,3584]{2,1,0:T(8,128)(2,1)} all-to-all(bf16[32,18,3584]{2,1,0:T(8,128)(2,1)S(1)} %bitcast.243), channel_id=1, replica_groups=mesh['section'=4,'expert'=32] {'expert'}, dimensions={0} | all-to-all | bytes 8257536 | tf_op jit(solution)/shard_map/all_to_all | solution.py:42
  304.2 7.3 reshape.1033
  311.5 8.1 fusion.15
  324.0 7.3 reshape.645
  331.3 7.1 all-to-all-start.3
  344.5 55.2 %all-to-all-done.3 = bf16[32,18,3584]{2,1,0:T(8,128)(2,1)} async-done(((bf16[32,18,3584]{2,1,0:T(8,128)(2,1)}), bf16[32,18,3584]{2,1,0:T(8,128)(2,1)}, u32[]{:S(2)}, u32[]{:S(2)}) %all-to-all-start.3) | async-done | bytes 4128800 | tf_op jit(solution)/shard_map/all_to_all | solution.py:50
  399.7 5.3 convert_reduce_fusion.2
  425.5 5.7 compare_and_fusion
  441.2 69.5 %all_to_all.42 = bf16[32,18,3584]{2,1,0:T(8,128)(2,1)} all-to-all(bf16[32,18,3584]{2,1,0:T(8,128)(2,1)S(1)} %bitcast.244), channel_id=1, replica_groups=mesh['section'=4,'expert'=32] {'expert'}, dimensions={0} | all-to-all | bytes 8257536 | tf_op jit(solution)/shard_map/all_to_all | solution.py:42
  510.6 7.3 reshape.1034
  518.0 8.1 fusion.18
  530.4 7.3 reshape.654
  537.7 7.2 all-to-all-start.5
  548.6 80.9 %all-to-all-done.5 = bf16[32,18,3584]{2,1,0:T(8,128)(2,1)} async-done(((bf16[32,18,3584]{2,1,0:T(8,128)(2,1)}), bf16[32,18,3584]{2,1,0:T(8,128)(2,1)}, u32[]{:S(2)}, u32[]{:S(2)}) %all-to-all-start.5) | async-done | bytes 4128800 | tf_op jit(solution)/shard_map/all_to_all | solution.py:50
  629.5 5.3 convert_reduce_fusion.1
  654.6 10.9 %collective-permute-done.5 = bf16[64,3584]{1,0:T(8,128)(2,1)S(1)} collective-permute-done((bf16[64,3584]{1,0:T(8,128)(2,1)S(1)}, bf16[64,3584]{1,0:T(8,128)(2,1)S(1)}, u32[]{:S(2)}, u32[]{:S(2)}) %collective-permute-start.5) | collective-permute-done | bytes 458784 | tf_op jit(solution)/shard_map/ppermute | solution.py:15
  673.1 62.2 %all_to_all.43 = bf16[32,18,3584]{2,1,0:T(8,128)(2,1)} all-to-all(bf16[32,18,3584]{2,1,0:T(8,128)(2,1)S(1)} %bitcast.245), channel_id=1, replica_groups=mesh['section'=4,'expert'=32] {'expert'}, dimensions={0} | all-to-all | bytes 8257536 | tf_op jit(solution)/shard_map/all_to_all | solution.py:42
  735.3 7.3 reshape.1035
  742.7 8.1 fusion.21
  755.1 7.3 reshape.663
  762.4 6.8 all-to-all-start.7
  772.8 60.6 %all-to-all-done.7 = bf16[32,18,3584]{2,1,0:T(8,128)(2,1)} async-done(((bf16[32,18,3584]{2,1,0:T(8,128)(2,1)}), bf16[32,18,3584]{2,1,0:T(8,128)(2,1)}, u32[]{:S(2)}, u32[]{:S(2)}) %all-to-all-start.7) | async-done | bytes 4128800 | tf_op jit(solution)/shard_map/all_to_all | solution.py:50
  833.4 5.3 convert_reduce_fusion
  (233 shorter events, 146.7 us)
Async XLA Ops:
  0.0 127.7 %copy-start = (f32[1,3584,8]{1,2,0:T(8,128)S(1)}, f32[1,3584,8]{1,2,0:T(8,128)}, u32[]{:S(2)}) copy-start(f32[1,3584,8]{1,2,0:T(8,128)} %param.31) | copy-start | bytes 344068
  12.4 115.3 %copy-start.9 = (f32[3584]{0:T(1024)}, f32[3584]{0:T(1024)S(1)}, u32[]{:S(2)}) copy-start(f32[3584]{0:T(1024)S(1)} %reduce.16) | copy-start | bytes 43012
  101.0 8.1 copy-start.36
  120.7 75.5 %all-to-all-start.1 = ((bf16[32,18,3584]{2,1,0:T(8,128)(2,1)}), bf16[32,18,3584]{2,1,0:T(8,128)(2,1)}, u32[]{:S(2)}, u32[]{:S(2)}) async-start(bf16[32,18,3584]{2,1,0:T(8,128)(2,1)} %reshape.637), calls=%async_computation.1 | async-start | bytes 11010048 | tf_op jit(solution)/shard_map/all_to_all | solution.py:50
  209.9 23.0 %copy-start.10 = (f32[3584]{0:T(1024)S(1)}, f32[3584]{0:T(1024)}, u32[]{:S(2)}) copy-start(f32[3584]{0:T(1024)} %copy-done.9) | copy-start | bytes 43012
  213.8 13.0 %collective-permute-start = (bf16[64,3584]{1,0:T(8,128)(2,1)S(1)}, bf16[64,3584]{1,0:T(8,128)(2,1)S(1)}, u32[]{:S(2)}, u32[]{:S(2)}) collective-permute-start(bf16[64,3584]{1,0:T(8,128)(2,1)S(1)} %fusion.77), channel_id=1, source_target_pairs={{0,32},{32,64},{64,96},{1,33},{33,65},{65,97},{2,34},{34,66},{66,9... | collective-permute-start | bytes 1376264 | tf_op jit(solution)/shard_map/ppermute | solution.py:15
  221.3 11.3 %collective-permute-start.1 = (bf16[64,3584]{1,0:T(8,128)(2,1)S(1)}, bf16[64,3584]{1,0:T(8,128)(2,1)S(1)}, u32[]{:S(2)}, u32[]{:S(2)}) collective-permute-start(bf16[64,3584]{1,0:T(8,128)(2,1)S(1)} %fusion.77), channel_id=1, source_target_pairs={{32,0},{64,32},{96,64},{33,1},{65,33},{97,65},{34,2},{66,34},{98,6... | collective-permute-start | bytes 1376264 | tf_op jit(solution)/shard_map/ppermute | solution.py:15
  311.5 8.1 copy-start.37
  331.3 7.4 copy-start.18
  331.3 7.6 copy-start.20
  331.3 8.4 copy-start.33
  331.3 68.5 %all-to-all-start.3 = ((bf16[32,18,3584]{2,1,0:T(8,128)(2,1)}), bf16[32,18,3584]{2,1,0:T(8,128)(2,1)}, u32[]{:S(2)}, u32[]{:S(2)}) async-start(bf16[32,18,3584]{2,1,0:T(8,128)(2,1)} %reshape.645), calls=%async_computation.3 | async-start | bytes 11010048 | tf_op jit(solution)/shard_map/all_to_all | solution.py:50
  413.6 10.8 %copy-start.26 = (s32[128]{0:T(128)S(1)}, s32[128]{0:T(128)}, u32[]{:S(2)}) copy-start(s32[128]{0:T(128)} %eq.148) | copy-start | bytes 1540
  413.6 10.9 %copy-start.16 = (s32[1,1,64,2]{3,2,1,0:T(8,128)S(1)}, s32[1,1,64,2]{3,2,1,0:T(8,128)}, u32[]{:S(2)}) copy-start(s32[1,1,64,2]{3,2,1,0:T(8,128)} %copy-done.15) | copy-start | bytes 1540
  413.6 11.1 %copy-start.14 = (s32[1,1,64,2]{3,2,1,0:T(8,128)S(1)}, s32[1,1,64,2]{3,2,1,0:T(8,128)}, u32[]{:S(2)}) copy-start(s32[1,1,64,2]{3,2,1,0:T(8,128)} %copy-done.13) | copy-start | bytes 1540
  413.6 11.2 %copy-start.17 = (s32[128,8]{1,0:T(8,128)S(1)}, s32[128,8]{1,0:T(8,128)}, u32[]{:S(2)}) copy-start(s32[128,8]{1,0:T(8,128)} %fusion.91) | copy-start | bytes 12292
  413.6 11.6 %copy-start.25 = (s32[128]{0:T(128)S(1)}, s32[128]{0:T(128)}, u32[]{:S(2)}) copy-start(s32[128]{0:T(128)} %copy-done.24) | copy-start | bytes 1540
  417.4 16.5 %copy-start.11 = (f32[3584]{0:T(1024)S(1)}, f32[3584]{0:T(1024)}, u32[]{:S(2)}) copy-start(f32[3584]{0:T(1024)} %copy-done.9) | copy-start | bytes 43012
  417.6 16.3 %copy-start.5 = (bf16[64,3584]{1,0:T(8,128)(2,1)}, bf16[64,3584]{1,0:T(8,128)(2,1)S(1)}, u32[]{:S(2)}) copy-start(bf16[64,3584]{1,0:T(8,128)(2,1)S(1)} %get-tuple-element.128) | copy-start | bytes 1376260
  417.6 13.7 %collective-permute-start.2 = (bf16[64,3584]{1,0:T(8,128)(2,1)S(1)}, bf16[64,3584]{1,0:T(8,128)(2,1)S(1)}, u32[]{:S(2)}, u32[]{:S(2)}) collective-permute-start(bf16[64,3584]{1,0:T(8,128)(2,1)S(1)} %get-tuple-element.128), channel_id=1, source_target_pairs={{0,32},{32,64},{64,96},{1,33},{33,65},{65,97},{2,34},{34,66},{66,9... | collective-permute-start | bytes 1376264 | tf_op jit(solution)/shard_map/ppermute | solution.py:15
  422.3 11.3 %collective-permute-start.3 = (bf16[64,3584]{1,0:T(8,128)(2,1)S(1)}, bf16[64,3584]{1,0:T(8,128)(2,1)S(1)}, u32[]{:S(2)}, u32[]{:S(2)}) collective-permute-start(bf16[64,3584]{1,0:T(8,128)(2,1)S(1)} %get-tuple-element.128), channel_id=1, source_target_pairs={{32,0},{64,32},{96,64},{33,1},{65,33},{97,65},{34,2},{66,34},{98,6... | collective-permute-start | bytes 1376264 | tf_op jit(solution)/shard_map/ppermute | solution.py:15
  518.0 8.1 copy-start.38
  537.7 7.2 copy-start.28
  537.7 8.1 copy-start.6
  537.7 91.8 %all-to-all-start.5 = ((bf16[32,18,3584]{2,1,0:T(8,128)(2,1)}), bf16[32,18,3584]{2,1,0:T(8,128)(2,1)}, u32[]{:S(2)}, u32[]{:S(2)}) async-start(bf16[32,18,3584]{2,1,0:T(8,128)(2,1)} %reshape.654), calls=%async_computation.5 | async-start | bytes 11010048 | tf_op jit(solution)/shard_map/all_to_all | solution.py:50
  647.1 18.8 %copy-start.12 = (f32[3584]{0:T(1024)S(1)}, f32[3584]{0:T(1024)}, u32[]{:S(2)}) copy-start(f32[3584]{0:T(1024)} %copy-done.9) | copy-start | bytes 43012
  647.3 22.6 %copy-start.7 = (bf16[64,3584]{1,0:T(8,128)(2,1)}, bf16[64,3584]{1,0:T(8,128)(2,1)S(1)}, u32[]{:S(2)}) copy-start(bf16[64,3584]{1,0:T(8,128)(2,1)S(1)} %get-tuple-element.116) | copy-start | bytes 1376260
  647.3 7.3 collective-permute-start.4
  649.2 16.3 %collective-permute-start.5 = (bf16[64,3584]{1,0:T(8,128)(2,1)S(1)}, bf16[64,3584]{1,0:T(8,128)(2,1)S(1)}, u32[]{:S(2)}, u32[]{:S(2)}) collective-permute-start(bf16[64,3584]{1,0:T(8,128)(2,1)S(1)} %get-tuple-element.116), channel_id=1, source_target_pairs={{32,0},{64,32},{96,64},{33,1},{65,33},{97,65},{34,2},{66,34},{98,6... | collective-permute-start | bytes 1376264 | tf_op jit(solution)/shard_map/ppermute | solution.py:15
  742.7 8.1 copy-start.39
  762.4 7.7 copy-start.8
  762.4 71.0 %all-to-all-start.7 = ((bf16[32,18,3584]{2,1,0:T(8,128)(2,1)}), bf16[32,18,3584]{2,1,0:T(8,128)(2,1)}, u32[]{:S(2)}, u32[]{:S(2)}) async-start(bf16[32,18,3584]{2,1,0:T(8,128)(2,1)} %reshape.663), calls=%async_computation.7 | async-start | bytes 11010048 | tf_op jit(solution)/shard_map/all_to_all | solution.py:50
  (18 other events, 54.5 us)
where the time goes:
time: 862 us; the launch traced here: 853 us
  waiting for transfers between devices  289 us (34%)
  blocking collectives  268 us (31%)
  local copies, waits for them, and re-layouts  118 us (14%)
  other arithmetic  67.8 us (8%)
  matrix products  57.3 us (7%)
  starting transfers between devices  48.4 us (6%)
    all_to_all x4, blocking collectives, run_layer(): lax.all_to_all(outgoing, 'expert', split_axis=0, concat_axis=0, tiled=True)  268 us
    all_to_all x4, waiting for transfers between devices, run_layer(): lax.all_to_all(computed, 'expert', split_axis=0, concat_axis=0, tiled=True)  263 us
    dot_general x4, matrix products, run_layer(): jnp.einsum('rd,gdf->grf', flat_rows, gate_up, preferred_element_type=jnp....  32.4 us
    reshape x4, local copies, waits for them, and re-layouts, run_layer(): flat_rows = arrived.reshape(-1, D)  29.4 us
    reshape x4, local copies, waits for them, and re-layouts, run_layer(): computed = partial_out.reshape(senders, count, D)  29.1 us
    all_to_all x4, starting transfers between devices, run_layer(): lax.all_to_all(computed, 'expert', split_axis=0, concat_axis=0, tiled=True)  27.8 us
    ppermute x6, waiting for transfers between devices, shifted(): lax.ppermute(value, axis, [(source, source + steps) for source in range(l...  25.6 us
    reduce_sum x4, other arithmetic, run_layer(): jnp.sum(back.reshape(EXPERTS, pieces, CAP, D).astype(jnp.float32), axis=1)  21 us
  transfers between devices with their start and end apart: 10, of which 9 were waited for; matrix products, arithmetic and copies ran while one was open for 3% of the time, Pallas kernels for 0%

commit v1 on v0

v1 whole, which is shorter than its diff:
```python
import jax
import jax.numpy as jnp
from jax import lax
from jax.experimental import pallas as pl
from jax.experimental.pallas import tpu as pltpu
from jax.sharding import PartitionSpec as P

MESH = pl.DeviceIdType.MESH
BF, F32, I32 = jnp.bfloat16, jnp.float32, jnp.int32

D = 3584
EXPERTS = 8
HALF = D // 2
BLK = 256
NBLK = HALF // BLK
WIDE = HALF + BLK
TOK = 64
HID = 512
ROWS = 256
XROWS = 288
LOST = 99.0


def iota(shape, dim):
    return lax.broadcasted_iota(I32, shape, dim)


def nt(a, b):
    return lax.dot_general(a, b, (((1,), (1,)), ((), ())), preferred_element_type=F32)


def mm(a, b):
    return jnp.dot(a, b, preferred_element_type=F32)


def kernel(
    order_ref, batches_ref, gain_ref, router_ref, routes_ref, caps_ref, w_in_hbm, w_down_hbm, out_ref,
    w_in, w_down, u_buf, normed, onehot, rk, gates, sel, pack,
    nb, x_buf, sa, sb, hidden, ext_out, out_buf, ra1, sa2, ra2, rb, sb2, rb2, acc_b,
    w_sem, rk_send, rk_recv, g_send, g_recv, nb_send, nb_recv, a1_send, a1_recv, a2_send, a2_recv, b_send, b_recv,
    rb_send, rb_recv, ra1_send, ra1_recv, ra2_send, ra2_recv, rb2_send, rb2_recv, u_send, u_recv,
):
    s, me = lax.axis_index("section"), lax.axis_index("expert")
    x, z, y = me // 16, lax.rem(me // 4, 4), lax.rem(me, 4)
    outer = jnp.logical_or(s == 0, s == 3)

    def chip(dx, dz, dy, at=None):
        ex = lax.rem(x + dx, 2) * 16 + lax.rem(z + dz + 4, 4) * 4 + lax.rem(y + dy, 4)
        return (s if at is None else at, ex)

    def send(src, dst, ssem, rsem, to):
        pltpu.make_async_remote_copy(
            src_ref=src, dst_ref=dst, send_sem=ssem, recv_sem=rsem, device_id=to, device_id_type=MESH
        ).start()

    def got(ref, sem):
        pltpu.make_async_remote_copy(
            src_ref=ref, dst_ref=ref, send_sem=sem, recv_sem=sem, device_id=chip(0, 0, 1), device_id_type=MESH
        ).wait_recv()

    def sent(ref, sem):
        pltpu.make_async_remote_copy(
            src_ref=ref, dst_ref=ref, send_sem=sem, recv_sem=sem, device_id=chip(0, 0, 1), device_id_type=MESH
        ).wait_send()

    offs = [(j % 2, (j // 2) * 2 + c) for c in range(2) for j in range(4)]

    copy_in = pltpu.make_async_copy(w_in_hbm, w_in, w_sem.at[0])
    copy_down = pltpu.make_async_copy(w_down_hbm, w_down, w_sem.at[1])
    copy_in.start()
    copy_down.start()

    barrier = pltpu.get_barrier_semaphore()
    for dx, dz in offs[1:]:
        pl.semaphore_signal(barrier, inc=1, device_id=chip(dx, dz, 0), device_id_type=MESH)
    for m in (1, 2, 3):
        pl.semaphore_signal(barrier, inc=1, device_id=chip(0, 0, m), device_id_type=MESH)
    for ds in (1, 3):
        pl.semaphore_signal(barrier, inc=1, device_id=(lax.rem(s + ds, 4), me), device_id_type=MESH)

    row, lane = iota((128, 128), 0), iota((128, 128), 1)
    o = row // 16
    dz_of = lax.rem(o // 2, 2) * 2 + o // 4
    expert_of = lax.rem(x + lax.rem(o, 2), 2) * 4 + lax.rem(z + dz_of, 4)
    onehot[...] = (lane == expert_of).astype(BF)
    r, c = iota((224, 256), 0), iota((224, 256), 1)
    sel[...] = (c == lax.rem(r, 32) * 8 + r // 32).astype(BF)
    r, c = iota((256, 224), 0), iota((256, 224), 1)
    pack[...] = (r == lax.rem(c, 32) * 8 + c // 32).astype(BF)
    lower = (iota((TOK, TOK), 0) > iota((TOK, TOK), 1)).astype(BF)
    gates[:, 0] = jnp.zeros((2, TOK, 128), BF)
    rk[0] = jnp.zeros((2, TOK, 128), BF)

    def named(step):
        direction = jnp.where(s < 2, step, 1 - step)
        pair = routes_ref[direction]
        number = iota((TOK, EXPERTS), 1)
        return jnp.logical_or(pair[:, 0:1] == number, pair[:, 1:2] == number)

    for step in range(2):
        names = named(step)
        rank = mm(lower, names.astype(F32).astype(BF))
        kept = jnp.logical_and(names, rank < caps_ref[...].astype(F32))
        rk[0, step, :, 0:EXPERTS] = jnp.where(kept, rank, LOST).astype(BF)

    @pl.when(outer)
    def _():
        u_buf[0] = batches_ref[order_ref[jnp.where(s == 0, 0, 1)]]

    pl.semaphore_wait(barrier, 12)
    for m in (1, 2, 3):
        send(rk.at[0], rk.at[4 - m], rk_send, rk_recv, chip(0, 0, m))

    def layer(step, carry):
        direction = jnp.where(s < 2, step, 1 - step)

        @pl.when(jnp.logical_not(jnp.logical_and(step == 0, outer)))
        def _():
            got(u_buf.at[step], u_recv.at[step])

        total = jnp.zeros((TOK, 512), F32)
        for i in range(D // 512):
            v = u_buf[step, :, i * 512:(i + 1) * 512].astype(F32)
            total = total + v * v
        inv = lax.rsqrt(jnp.sum(total, axis=1, keepdims=True) * (1.0 / D) + 1e-06)

        def norm_half(first):
            for i in range(first, first + HALF, 256):
                v = u_buf[step, :, i:i + 256].astype(F32)
                normed[:, i:i + 256] = (v * inv * gain_ref[:, i:i + 256]).astype(BF)

        norm_half(HALF)
        for m in (1, 2, 3):
            send(normed.at[:, HALF:D], nb.at[step, 3 - m], nb_send, nb_recv.at[step, 3 - m], chip(0, 0, m))
        norm_half(0)

        def packer(ranks):
            rt = nt(onehot[...], ranks)
            main = (rt == lax.rem(iota((128, TOK), 0), 16).astype(F32)).astype(BF)
            rt7 = nt(onehot[...], jnp.concatenate([ranks] * NBLK, axis=0))
            rw, cl = iota((128, TOK * NBLK), 0), iota((128, TOK * NBLK), 1)
            want = (16 + lax.rem(rw, 16) // 8).astype(F32)
            ext = jnp.logical_and(rt7 == want, lax.rem(rw, 8) == cl // TOK).astype(BF)
            return main, ext

        def packed(ranks, source, put):
            main, ext = packer(ranks)
            for i in range(NBLK):
                put(i * BLK, mm(main, source(i)).astype(BF))
            stack = jnp.concatenate([source(i) for i in range(NBLK)], axis=0)
            put(HALF, mm(ext, stack).astype(BF))

        def put_a(at, v):
            x_buf[step, 0, 0:16, at:at + BLK] = v[0:16]
            sa[:, :, at:at + BLK] = v[16:128].reshape(7, 16, BLK)

        packed(rk[0, step], lambda i: normed[:, i * BLK:(i + 1) * BLK], put_a)
        for i, (dx, dz) in enumerate(offs):
            if i:
                ch, j = i // 4, i % 4
                send(
                    sa.at[i - 1], x_buf.at[step, ch, j * 64:j * 64 + 16, 0:WIDE],
                    a1_send, a1_recv.at[step, i], chip(dx, dz, 0),
                )

        def second(d):
            def put_b(at, v):
                x_buf[step, 0, d * 16:d * 16 + 16, WIDE + at:WIDE + at + BLK] = v[0:16]
                sb[:, d * 16:d * 16 + 16, at:at + BLK] = v[16:128].reshape(7, 16, BLK)

            if d == 0:
                packed(rk[0, step], lambda i: normed[:, HALF + i * BLK:HALF + (i + 1) * BLK], put_b)
            else:
                packed(rk[d, step], lambda i: nb[step, d - 1, :, i * BLK:(i + 1) * BLK], put_b)
            for i, (dx, dz) in enumerate(offs):
                if i:
                    ch, j = i // 4, i % 4
                    at = j * 64 + d * 16
                    send(
                        sb.at[i - 1, d * 16:d * 16 + 16], x_buf.at[step, ch, at:at + 16, WIDE:2 * WIDE],
                        b_send, b_recv.at[step, ch], chip(dx, dz, 0),
                    )

        def forward(i):
            ch, j = i // 4, i % 4
            if i:
                got(x_buf.at[step, ch, j * 64:j * 64 + 16, 0:WIDE], a1_recv.at[step, i])
            for m in (1, 3, 2):
                at = j * 64 + (4 - m) * 16
                send(
                    x_buf.at[step, ch, j * 64:j * 64 + 16, 0:WIDE], x_buf.at[step, ch, at:at + 16, 0:WIDE],
                    a2_send, a2_recv.at[step, ch], chip(0, 0, m),
                )

        forward(0)
        second(0)
        forward(1)
        forward(2)

        @pl.when(step == 0)
        def _():
            got(rk.at[1:4], rk_recv)

        for d in (1, 3):
            got(nb.at[step, d - 1], nb_recv.at[step, d - 1])
            second(d)
            forward(d + 2)
        forward(4)
        got(nb.at[step, 1], nb_recv.at[step, 1])
        second(2)
        forward(6)
        forward(7)

        router = router_ref[...]
        high = router.astype(BF)
        low = (router - high.astype(F32)).astype(BF)
        scores = jax.nn.sigmoid(mm(normed[...], high) + mm(normed[...], low))
        chosen = jnp.sum(jnp.where(named(step), scores, 0.0), axis=1, keepdims=True)
        gates[step, 0, :, 0:EXPERTS] = (2.5 * scores / chosen).astype(BF)
        for m in (1, 2, 3):
            send(gates.at[step, 0], gates.at[step, 4 - m], g_send, g_recv.at[step], chip(0, 0, m))

        @pl.when(step == 0)
        def _():
            copy_in.wait()
            copy_down.wait()

        for ch in range(2):
            xs = x_buf.at[step, ch]
            ob = out_buf.at[ch]
            got(x_buf.at[step, ch, 0:192, 0:WIDE], a2_recv.at[step, ch])
            got(x_buf.at[step, ch, 0:192 + 64 * ch, 0:WIDE], b_recv.at[step, ch])
            for p in range(2):
                spread = mm(sel[...], xs[0:ROWS, p * WIDE + HALF:(p + 1) * WIDE]).astype(BF)
                for i in range(NBLK):
                    xs[ROWS:XROWS, p * WIDE + i * BLK:p * WIDE + (i + 1) * BLK] = spread[i * 32:(i + 1) * 32]

            def up(n, carry):
                cols = pl.ds(pl.multiple_of(n * 256, 256), 256)
                g, v = (
                    mm(xs[:, 0:HALF], w_in[q, 0:HALF, cols]) + mm(xs[:, WIDE:WIDE + HALF], w_in[q, HALF:D, cols])
                    for q in range(2)
                )
                hidden[:, cols] = (jax.nn.silu(g) * v).astype(BF)
                return carry

            lax.fori_loop(0, HID // 256, up, 0)

            for p in (1, 0):
                def down(n, carry):
                    v = mm(hidden[...], w_down[:, pl.ds(pl.multiple_of(p * HALF + n * BLK, BLK), BLK)]).astype(BF)
                    ob[0:ROWS, pl.ds(pl.multiple_of(p * WIDE + n * BLK, BLK), BLK)] = v[0:ROWS]
                    ext_out[pl.ds(pl.multiple_of(n * 32, 32), 32), :] = v[ROWS:XROWS]
                    return carry

                lax.fori_loop(0, NBLK, down, 0)
                ob[0:ROWS, p * WIDE + HALF:(p + 1) * WIDE] = mm(pack[...], ext_out[...]).astype(BF)
                for j in range(4):
                    i = ch * 4 + j
                    dx, dz = offs[i]
                    if p == 1:
                        if i == 0:
                            rb[step, 0] = ob[0:64, WIDE:2 * WIDE]
                        else:
                            send(
                                ob.at[j * 64:j * 64 + 64, WIDE:2 * WIDE], rb.at[step, i],
                                rb_send, rb_recv.at[step], chip(dx, -dz, 0),
                            )
                    else:
                        for m in (1, 3, 2):
                            send(
                                ob.at[j * 64 + m * 16:j * 64 + m * 16 + 16, 0:WIDE],
                                ra1.at[step, ch, 3 - m, j * 16:j * 16 + 16],
                                ra1_send, ra1_recv.at[step, ch], chip(0, 0, m),
                            )

        for ch in range(2):
            got(ra1.at[step, ch], ra1_recv.at[step, ch])
            for j in range(4):
                i = ch * 4 + j
                dx, dz = offs[i]
                v = out_buf[ch, j * 64:j * 64 + 16, 0:WIDE].astype(F32)
                for m in range(3):
                    v = v + ra1[step, ch, m, j * 16:j * 16 + 16].astype(F32)
                if i == 0:
                    ra2[step, 0] = v.astype(BF)
                else:
                    sa2[i - 1] = v.astype(BF)
                    send(sa2.at[i - 1], ra2.at[step, i], ra2_send, ra2_recv.at[step], chip(dx, -dz, 0))

        def weights(ranks, gate):
            rt, gt = nt(ranks, onehot[...]), nt(gate, onehot[...])
            main = jnp.where(rt == lax.rem(iota((TOK, 128), 1), 16).astype(F32), gt, 0.0).astype(BF)
            rw, cl = iota((TOK * NBLK, 128), 0), iota((TOK * NBLK, 128), 1)
            want = (16 + lax.rem(cl, 16) // 8).astype(F32)
            take = jnp.logical_and(
                jnp.concatenate([rt] * NBLK, axis=0) == want, lax.rem(cl, 8) == rw // TOK
            )
            return main, jnp.where(take, jnp.concatenate([gt] * NBLK, axis=0), 0.0).astype(BF)

        got(gates.at[step, 1:4], g_recv.at[step])
        got(rb.at[step, 1:8], rb_recv.at[step])
        for d in (2, 1, 3, 0):
            main, ext = weights(rk[d, step], gates[step, d])
            over = mm(ext, rb[step, :, d * 16:d * 16 + 16, HALF:WIDE].reshape(128, BLK))
            for i in range(NBLK):
                v = mm(main, rb[step, :, d * 16:d * 16 + 16, i * BLK:(i + 1) * BLK].reshape(128, BLK))
                v = v + over[i * TOK:(i + 1) * TOK]
                if d == 0:
                    acc_b[:, i * BLK:(i + 1) * BLK] = v
                else:
                    sb2[d - 1, :, i * BLK:(i + 1) * BLK] = v.astype(BF)
            if d:
                send(sb2.at[d - 1], rb2.at[step, 3 - d], rb2_send, rb2_recv.at[step], chip(0, 0, d))

        got(ra2.at[step, 1:8], ra2_recv.at[step])
        main, ext = weights(rk[0, step], gates[step, 0])
        over = mm(ext, ra2[step, :, :, HALF:WIDE].reshape(128, BLK))
        for i in range(NBLK):
            cols = slice(i * BLK, (i + 1) * BLK)
            v = mm(main, ra2[step, :, :, cols].reshape(128, BLK)) + over[i * TOK:(i + 1) * TOK]
            out_ref[direction, :, cols] = (u_buf[step, :, cols].astype(F32) + v).astype(BF)
        got(rb2.at[step], rb2_recv.at[step])
        for i in range(NBLK):
            cols, at = slice(i * BLK, (i + 1) * BLK), slice(HALF + i * BLK, HALF + (i + 1) * BLK)
            v = acc_b[:, cols]
            for m in range(3):
                v = v + rb2[step, m, :, cols].astype(F32)
            out_ref[direction, :, at] = (u_buf[step, :, at].astype(F32) + v).astype(BF)

        target = jnp.where(direction == 0, s + 1, s - 1)
        relays = jnp.logical_and(target >= 0, target <= 3)
        target_step = jnp.where(jnp.logical_and(step == 0, outer), 0, 1)

        @pl.when(relays)
        def _():
            send(out_ref.at[direction], u_buf.at[target_step], u_send, u_recv.at[target_step], (target, me))

        sent(nb.at[step], nb_send)
        sent(sa, a1_send)
        sent(out_buf.at[:, 0:192, 0:WIDE], a2_send)
        sent(sb, b_send)
        sent(gates.at[step, 1:4], g_send)
        sent(sb, rb_send)
        sent(out_buf.at[:, 0:192, 0:WIDE], ra1_send)
        sent(sa2, ra2_send)
        sent(sb2, rb2_send)

        @pl.when(relays)
        def _():
            sent(u_buf.at[step], u_send)

        return carry

    lax.fori_loop(0, 2, layer, 0)
    sent(rk.at[1:4], rk_send)


def local(batches, order, gains, router, routes, caps, w_in, w_down):
    vmem, hbm = pl.BlockSpec(memory_space=pltpu.VMEM), pl.BlockSpec(memory_space=pl.ANY)
    dma = pltpu.SemaphoreType.DMA
    out = pl.pallas_call(
        kernel,
        out_shape=jax.ShapeDtypeStruct((2, TOK, D), BF),
        in_specs=[pl.BlockSpec(memory_space=pltpu.SMEM), vmem, vmem, vmem, vmem, vmem, hbm, hbm],
        out_specs=vmem,
        scratch_shapes=[
            pltpu.VMEM((2, D, HID), BF),
            pltpu.VMEM((HID, D), BF),
            pltpu.VMEM((2, TOK, D), BF),
            pltpu.VMEM((TOK, D), BF),
            pltpu.VMEM((128, 128), BF),
            pltpu.VMEM((4, 2, TOK, 128), BF),
            pltpu.VMEM((2, 4, TOK, 128), BF),
            pltpu.VMEM((224, 256), BF),
            pltpu.VMEM((256, 224), BF),
            pltpu.VMEM((2, 3, TOK, HALF), BF),
            pltpu.VMEM((2, 2, XROWS, 2 * WIDE), BF),
            pltpu.VMEM((7, 16, WIDE), BF),
            pltpu.VMEM((7, 64, WIDE), BF),
            pltpu.VMEM((XROWS, HID), BF),
            pltpu.VMEM((224, 256), BF),
            pltpu.VMEM((2, ROWS, 2 * WIDE), BF),
            pltpu.VMEM((2, 2, 3, 64, WIDE), BF),
            pltpu.VMEM((7, 16, WIDE), BF),
            pltpu.VMEM((2, 8, 16, WIDE), BF),
            pltpu.VMEM((2, 8, 64, WIDE), BF),
            pltpu.VMEM((3, TOK, HALF), BF),
            pltpu.VMEM((2, 3, TOK, HALF), BF),
            pltpu.VMEM((TOK, HALF), F32),
            dma((2,)),
            dma, dma,
            dma, dma((2,)),
            dma, dma((2, 3)),
            dma, dma((2, 8)),
            dma, dma((2, 2)),
            dma, dma((2, 2)),
            dma, dma((2,)),
            dma, dma((2, 2)),
            dma, dma((2,)),
            dma, dma((2,)),
            dma, dma((2,)),
        ],
        compiler_params=pltpu.CompilerParams(
            collective_id=0, has_side_effects=True, vmem_limit_bytes=60 << 20
        ),
        name="relay",
    )(order, batches, gains, router[0], routes[0], caps, w_in[0], w_down[0])
    return out[None]


def solution(mesh):
    placed = (
        P(None, "expert", None),
        P(),
        P("section", None),
        P("section", None, None),
        P("section", None, "expert", None),
        P("section", None),
        P("section", None, None, "expert"),
        P("section", "expert", None),
    )
    return jax.shard_map(
        local,
        mesh=mesh,
        in_specs=placed,
        out_specs=P("section", None, "expert", None),
        check_vma=False,
    )
```

time: 862 us -> 224 us (0.26)
  the two profiles are of different devices: /device:TPU:19 before, /device:TPU:0 now
where the time goes in v1:
time: 224 us
  Pallas kernels  217 us (97%)
  local copies, waits for them, and re-layouts  6.27 us (3%)
    pallas_call x1, Pallas kernels, local(): pl.pallas_call(kernel, out_shape=jax.ShapeDtypeStruct((2, TOK, D), BF), i...  217 us
    unnamed x3, local copies, waits for them, and re-layouts  6.27 us

profile of v1, /device:TPU:0, one launch (start us, length us, event | category | flops | bytes accessed | tf_op | source)
XLA Modules:
  0.0 223.7 jit_solution(8481794855706571559)
XLA Ops:
  0.0 1.4 copy.10
  1.4 2.7 %copy.9 = f32[1,3584,8]{2,1,0:T(8,128)} copy(f32[1,3584,8]{1,2,0:T(8,128)} %param.11) | data formatting | bytes 229376 | tf_op args[3]
  4.1 217.5 %relay.1 = bf16[2,64,3584]{2,1,0:T(8,128)(2,1)} custom-call(s32[4]{0:T(128)} %order_ref.1, bf16[4,64,3584]{2,1,0:T(8,128)(2,1)} %batches_ref.1, f32[1,3584]{1,0:T(1,128)} %gain_ref.1, f32[3584,8]{1,0:T(8,128)} %bitcast.6, s32[2,64,2]{2,1,0:T(8,128)} %bitcast.9, s32[1,8]{1,0:T(1,128)} %caps_ref.1, bf16[2,3584,512]{2,1,0:T(8,128)(2,1)} %bitcast.5, ...), custom_call_target="tpu_custom_call" | custom-call | tf_op jit(solution)/shard_map/relay/pallas_call | solution.py:362
  221.6 2.2 copy.12

commit v2 on v1

v2 whole, which is shorter than its diff:
```python
import jax
import jax.numpy as jnp
from jax import lax
from jax.experimental import pallas as pl
from jax.experimental.pallas import tpu as pltpu
from jax.sharding import PartitionSpec as P

MESH = pl.DeviceIdType.MESH
BF, F32, I32 = jnp.bfloat16, jnp.float32, jnp.int32

D = 3584
EXPERTS = 8
HALF = D // 2
BLK = 256
NBLK = HALF // BLK
WIDE = HALF + BLK
TOK = 64
HID = 512
ROWS = 256
XROWS = 288
LOST = 99.0


def iota(shape, dim):
    return lax.broadcasted_iota(I32, shape, dim)


def nt(a, b):
    return lax.dot_general(a, b, (((1,), (1,)), ((), ())), preferred_element_type=F32)


def mm(a, b):
    return jnp.dot(a, b, preferred_element_type=F32)


def kernel(
    order_ref, batches_ref, gain_ref, router_ref, routes_ref, caps_ref, w_in_hbm, w_down_hbm, out_ref,
    w_in, w_down, u_buf, normed, onehot, rk_own, rk_near, gates_own, gates_near, sel, pack,
    nb, x_buf, sa, sb, hidden, ext_out, out_buf, part, sa2, sn2, ra2, rn2, s3, r3,
    w_sem, rk_send, rk_recv, g_send, g_recv, nb_send, nb_recv, a1_send, a1_recv, b_send, b_recv, a2_send, a2_recv,
    part_send, part_recv, ra2_send, ra2_recv, rn2_send, rn2_recv, r3_send, r3_recv, u_send, u_recv,
):
    s, me = lax.axis_index("section"), lax.axis_index("expert")
    x, z, y = me // 16, lax.rem(me // 4, 4), lax.rem(me, 4)
    outer = jnp.logical_or(s == 0, s == 3)

    def chip(dx, dz, dy):
        return (s, lax.rem(x + dx, 2) * 16 + lax.rem(z + dz + 4, 4) * 4 + lax.rem(y + dy, 4))

    def send(src, dst, ssem, rsem, to):
        pltpu.make_async_remote_copy(
            src_ref=src, dst_ref=dst, send_sem=ssem, recv_sem=rsem, device_id=to, device_id_type=MESH
        ).start()

    def got(ref, sem):
        pltpu.make_async_remote_copy(
            src_ref=ref, dst_ref=ref, send_sem=sem, recv_sem=sem, device_id=chip(0, 0, 1), device_id_type=MESH
        ).wait_recv()

    def sent(ref, sem):
        pltpu.make_async_remote_copy(
            src_ref=ref, dst_ref=ref, send_sem=sem, recv_sem=sem, device_id=chip(0, 0, 1), device_id_type=MESH
        ).wait_send()

    offs = [(j % 2, (j // 2) * 2 + c) for c in range(2) for j in range(4)]
    toward, near = (1, 3), (3, 1)

    def lanes(p):
        return slice(p * WIDE, (p + 1) * WIDE)

    copy_in = pltpu.make_async_copy(w_in_hbm, w_in, w_sem.at[0])
    copy_down = pltpu.make_async_copy(w_down_hbm, w_down, w_sem.at[1])
    copy_in.start()
    copy_down.start()

    barrier = pltpu.get_barrier_semaphore()
    for dx, dz in offs[1:]:
        pl.semaphore_signal(barrier, inc=1, device_id=chip(dx, dz, 0), device_id_type=MESH)
    for m in (1, 3):
        pl.semaphore_signal(barrier, inc=1, device_id=chip(0, 0, m), device_id_type=MESH)
    for ds in (1, 3):
        pl.semaphore_signal(barrier, inc=1, device_id=(lax.rem(s + ds, 4), me), device_id_type=MESH)

    row, lane = iota((128, 128), 0), iota((128, 128), 1)
    o = row // 16
    dz_of = lax.rem(o // 2, 2) * 2 + o // 4
    expert_of = lax.rem(x + lax.rem(o, 2), 2) * 4 + lax.rem(z + dz_of, 4)
    onehot[...] = (lane == expert_of).astype(BF)
    r, c = iota((224, 256), 0), iota((224, 256), 1)
    sel[...] = (c == lax.rem(r, 32) * 8 + r // 32).astype(BF)
    r, c = iota((256, 224), 0), iota((256, 224), 1)
    pack[...] = (r == lax.rem(c, 32) * 8 + c // 32).astype(BF)
    lower = (iota((TOK, TOK), 0) > iota((TOK, TOK), 1)).astype(BF)
    eye = (iota((TOK, TOK), 0) == iota((TOK, TOK), 1)).astype(BF)
    gates_own[...] = jnp.zeros_like(gates_own)
    rk_own[...] = jnp.zeros_like(rk_own)

    def named(step):
        direction = jnp.where(s < 2, step, 1 - step)
        pair = routes_ref[direction]
        number = iota((EXPERTS, TOK), 0)
        names = jnp.logical_or(pair[0:1] == number, pair[1:2] == number)
        return names.astype(F32).astype(BF)

    for step in range(2):
        names = named(step)
        rank = nt(lower, names)
        kept = jnp.logical_and(nt(eye, names) > 0.5, rank < caps_ref[...].astype(F32))
        rk_own[step, :, 0:EXPERTS] = jnp.where(kept, rank, LOST).astype(BF)

    @pl.when(outer)
    def _():
        u_buf[0] = batches_ref[order_ref[jnp.where(s == 0, 0, 1)]]

    pl.semaphore_wait(barrier, 11)
    for p in range(2):
        send(rk_own, rk_near.at[p], rk_send, rk_recv, chip(0, 0, toward[p]))

    def layer(step, carry):
        direction = jnp.where(s < 2, step, 1 - step)

        @pl.when(jnp.logical_not(jnp.logical_and(step == 0, outer)))
        def _():
            got(u_buf.at[step], u_recv.at[step])

        total = jnp.zeros((TOK, 512), F32)
        for i in range(D // 512):
            v = u_buf[step, :, i * 512:(i + 1) * 512].astype(F32)
            total = total + v * v
        inv = lax.rsqrt(jnp.sum(total, axis=1, keepdims=True) * (1.0 / D) + 1e-06)
        for p in range(2):
            for i in range(p * HALF, (p + 1) * HALF, 256):
                v = u_buf[step, :, i:i + 256].astype(F32)
                normed[:, i:i + 256] = (v * inv * gain_ref[:, i:i + 256]).astype(BF)
            send(
                normed.at[:, p * HALF:(p + 1) * HALF], nb.at[step, p],
                nb_send, nb_recv.at[step, p], chip(0, 0, toward[p]),
            )

        def packer(ranks):
            rt = nt(onehot[...], ranks)
            main = (rt == lax.rem(iota((128, TOK), 0), 16).astype(F32)).astype(BF)
            rt7 = nt(onehot[...], jnp.concatenate([ranks] * NBLK, axis=0))
            rw, cl = iota((128, TOK * NBLK), 0), iota((128, TOK * NBLK), 1)
            want = (16 + lax.rem(rw, 16) // 8).astype(F32)
            ext = jnp.logical_and(rt7 == want, lax.rem(rw, 8) == cl // TOK).astype(BF)
            return main, ext

        def packed(tables, source, put):
            main, ext = tables
            for i in range(NBLK):
                put(i * BLK, mm(main, source(i)).astype(BF))
            stack = jnp.concatenate([source(i) for i in range(NBLK)], axis=0)
            put(HALF, mm(ext, stack).astype(BF))

        def send_own(i):
            (dx, dz), ch, j = offs[i], i // 4, i % 4
            send(sa.at[i - 1], x_buf.at[step, ch, j * 16:j * 16 + 16], a1_send, a1_recv.at[step, i], chip(dx, dz, 0))

        def send_near(p, i):
            (dx, dz), ch, at = offs[i], i // 4, near[p] * 64 + i % 4 * 16
            send(
                sb.at[p, i - 1], x_buf.at[step, ch, at:at + 16, lanes(p)],
                b_send, b_recv.at[step, p * 8 + i], chip(dx, dz, 0),
            )

        def forward_own(i):
            ch, j = i // 4, i % 4
            if i:
                got(x_buf.at[step, ch, j * 16:j * 16 + 16], a1_recv.at[step, i])
            for p in range(2):
                at = toward[p] * 64 + j * 16
                send(
                    x_buf.at[step, ch, j * 16:j * 16 + 16, lanes(p)], x_buf.at[step, ch, at:at + 16, lanes(p)],
                    a2_send, a2_recv.at[step, ch], chip(0, 0, near[p]),
                )

        def forward_near(p, i):
            ch, j = i // 4, i % 4
            at, to = near[p] * 64 + j * 16, 128 + j * 16
            if i:
                got(x_buf.at[step, ch, at:at + 16, lanes(p)], b_recv.at[step, p * 8 + i])
            send(
                x_buf.at[step, ch, at:at + 16, lanes(p)], x_buf.at[step, ch, to:to + 16, lanes(p)],
                a2_send, a2_recv.at[step, ch], chip(0, 0, toward[p]),
            )

        tables = packer(rk_own[step])
        for p in range(2):
            def put_own(at, v):
                x_buf[step, 0, 0:16, p * WIDE + at:p * WIDE + at + BLK] = v[0:16]
                sa[:, :, p * WIDE + at:p * WIDE + at + BLK] = v[16:128].reshape(7, 16, BLK)

            packed(tables, lambda i: normed[:, p * HALF + i * BLK:p * HALF + (i + 1) * BLK], put_own)
        for i in (1, 2, 3):
            send_own(i)
        forward_own(0)

        @pl.when(step == 0)
        def _():
            got(rk_near, rk_recv)

        for p in range(2):
            def put_near(at, v):
                first = near[p] * 64
                x_buf[step, 0, first:first + 16, p * WIDE + at:p * WIDE + at + BLK] = v[0:16]
                sb[p, :, :, at:at + BLK] = v[16:128].reshape(7, 16, BLK)

            tables = packer(rk_near[p, step])
            got(nb.at[step, p], nb_recv.at[step, p])
            packed(tables, lambda i: nb[step, p, :, i * BLK:(i + 1) * BLK], put_near)
            for i in (1, 2, 3):
                send_near(p, i)
            forward_near(p, 0)
        for i in (1, 2, 3):
            forward_own(i)
        for i in range(4, 8):
            send_own(i)
        for p in range(2):
            for i in (1, 2, 3):
                forward_near(p, i)
        for i in range(4, 8):
            for p in range(2):
                send_near(p, i)

        router = router_ref[...]
        high = router.astype(BF)
        low = (router - high.astype(F32)).astype(BF)
        scores = jax.nn.sigmoid(nt(normed[...], high) + nt(normed[...], low))
        chosen = jnp.sum(nt(eye, named(step)) * scores, axis=1, keepdims=True)
        gates_own[step, :, 0:EXPERTS] = (2.5 * scores / chosen).astype(BF)
        for p in range(2):
            send(gates_own.at[step], gates_near.at[step, p], g_send, g_recv.at[step], chip(0, 0, toward[p]))

        for i in range(4, 8):
            forward_own(i)

        @pl.when(step == 0)
        def _():
            copy_in.wait()
            copy_down.wait()

        def arrived(ch):
            got(x_buf.at[step, ch, 0:ROWS, 0:WIDE], a2_recv.at[step, ch])
            for p in range(2):
                spread = mm(sel[...], x_buf[step, ch, 0:ROWS, p * WIDE + HALF:(p + 1) * WIDE]).astype(BF)
                for i in range(NBLK):
                    cols = slice(p * WIDE + i * BLK, p * WIDE + (i + 1) * BLK)
                    x_buf[step, ch, ROWS:XROWS, cols] = spread[i * 32:(i + 1) * 32]

        def up(ch, n):
            cols = slice(n * 256, (n + 1) * 256)
            g, v = (
                mm(x_buf[step, ch, :, 0:HALF], w_in[q, 0:HALF, cols])
                + mm(x_buf[step, ch, :, WIDE:WIDE + HALF], w_in[q, HALF:D, cols])
                for q in range(2)
            )
            hidden[:, cols] = (jax.nn.silu(g) * v).astype(BF)

        def down(ch, p):
            def tile(n, carry):
                v = mm(hidden[...], w_down[:, pl.ds(pl.multiple_of(p * HALF + n * BLK, BLK), BLK)]).astype(BF)
                out_buf[ch, 0:ROWS, pl.ds(pl.multiple_of(p * WIDE + n * BLK, BLK), BLK)] = v[0:ROWS]
                ext_out[pl.ds(pl.multiple_of(n * 32, 32), 32), :] = v[ROWS:XROWS]
                return carry

            lax.fori_loop(0, NBLK, tile, 0)
            out_buf[ch, 0:ROWS, p * WIDE + HALF:(p + 1) * WIDE] = mm(pack[...], ext_out[...]).astype(BF)

        def send_part(ch, p, q):
            first, to = (128, near[p]) if q else (toward[p] * 64, toward[p])
            send(
                out_buf.at[ch, first:first + 64, lanes(p)], part.at[step, ch, p * 2 + q],
                part_send, part_recv.at[step, ch * 4 + p * 2 + q], chip(0, 0, to),
            )

        def back(ch, p, q):
            got(part.at[step, ch, p * 2 + q], part_recv.at[step, ch * 4 + p * 2 + q])
            for j in range(4):
                i = ch * 4 + j
                dx, dz = offs[i]
                first = near[p] * 64 * q + j * 16
                v = out_buf[ch, first:first + 16, lanes(p)].astype(F32)
                v = (v + part[step, ch, p * 2 + q, j * 16:j * 16 + 16].astype(F32)).astype(BF)
                if q and i:
                    sn2[p, i - 1] = v
                    send(sn2.at[p, i - 1], rn2.at[step, p, i], rn2_send, rn2_recv.at[step, p], chip(dx, -dz, 0))
                elif q:
                    rn2[step, p, 0] = v
                elif i:
                    sa2[i - 1, :, lanes(p)] = v
                    if p:
                        send(sa2.at[i - 1], ra2.at[step, i], ra2_send, ra2_recv.at[step], chip(dx, -dz, 0))
                else:
                    ra2[step, 0, :, lanes(p)] = v

        arrived(0)
        up(0, 0)
        for p in range(2):
            for i in range(4, 8):
                forward_near(p, i)
        up(0, 1)
        for p in range(2):
            down(0, p)
            send_part(0, p, 1)
            send_part(0, p, 0)
        arrived(1)
        up(1, 0)
        up(1, 1)
        back(0, 0, 1)
        down(1, 0)
        send_part(1, 0, 1)
        back(0, 1, 1)
        down(1, 1)
        send_part(1, 1, 1)
        send_part(1, 0, 0)
        send_part(1, 1, 0)
        back(0, 0, 0)
        back(0, 1, 0)
        for q in (1, 0):
            for p in range(2):
                back(1, p, q)

        def weights(ranks, gate):
            rt, gt = nt(ranks, onehot[...]), nt(gate, onehot[...])
            main = jnp.where(rt == lax.rem(iota((TOK, 128), 1), 16).astype(F32), gt, 0.0).astype(BF)
            rw, cl = iota((TOK * NBLK, 128), 0), iota((TOK * NBLK, 128), 1)
            want = (16 + lax.rem(cl, 16) // 8).astype(F32)
            take = jnp.logical_and(
                jnp.concatenate([rt] * NBLK, axis=0) == want, lax.rem(cl, 8) == rw // TOK
            )
            return main, jnp.where(take, jnp.concatenate([gt] * NBLK, axis=0), 0.0).astype(BF)

        def weighed(tables, source, put):
            main, ext = tables
            over = mm(ext, source(HALF))
            for i in range(NBLK):
                put(i * BLK, mm(main, source(i * BLK)) + over[i * TOK:(i + 1) * TOK])

        got(gates_near.at[step], g_recv.at[step])
        for p in range(2):
            def put_back(at, v):
                s3[p, :, at:at + BLK] = v.astype(BF)

            tables = weights(rk_near[p, step], gates_near[step, p])
            got(rn2.at[step, p, 1:8], rn2_recv.at[step, p])
            weighed(tables, lambda at: rn2[step, p, :, :, at:at + BLK].reshape(128, BLK), put_back)
            send(s3.at[p], r3.at[step, p], r3_send, r3_recv.at[step, p], chip(0, 0, near[p]))

        tables = weights(rk_own[step], gates_own[step])
        got(ra2.at[step, 1:8], ra2_recv.at[step])
        for p in range(2):
            got(r3.at[step, p], r3_recv.at[step, p])

            def put_out(at, v):
                cols = slice(p * HALF + at, p * HALF + at + BLK)
                v = v + r3[step, p, :, at:at + BLK].astype(F32)
                out_ref[direction, :, cols] = (u_buf[step, :, cols].astype(F32) + v).astype(BF)

            weighed(tables, lambda at: ra2[step, :, :, p * WIDE + at:p * WIDE + at + BLK].reshape(128, BLK), put_out)

        target = jnp.where(direction == 0, s + 1, s - 1)
        relays = jnp.logical_and(target >= 0, target <= 3)
        target_step = jnp.where(jnp.logical_and(step == 0, outer), 0, 1)

        @pl.when(relays)
        def _():
            send(out_ref.at[direction], u_buf.at[target_step], u_send, u_recv.at[target_step], (target, me))

        sent(nb.at[step], nb_send)
        sent(sa, a1_send)
        sent(sb, b_send)
        sent(x_buf.at[step, :, 0:ROWS, 0:WIDE], a2_send)
        sent(gates_near.at[step], g_send)
        sent(part.at[step], part_send)
        sent(sa2, ra2_send)
        sent(sn2, rn2_send)
        sent(s3, r3_send)

        @pl.when(relays)
        def _():
            sent(u_buf.at[step], u_send)

        return carry

    lax.fori_loop(0, 2, layer, 0)
    sent(rk_near, rk_send)


def local(batches, order, gains, router, routes, caps, w_in, w_down):
    vmem, hbm = pl.BlockSpec(memory_space=pltpu.VMEM), pl.BlockSpec(memory_space=pl.ANY)
    dma = pltpu.SemaphoreType.DMA
    out = pl.pallas_call(
        kernel,
        out_shape=jax.ShapeDtypeStruct((2, TOK, D), BF),
        in_specs=[pl.BlockSpec(memory_space=pltpu.SMEM), vmem, vmem, vmem, vmem, vmem, hbm, hbm],
        out_specs=vmem,
        scratch_shapes=[
            pltpu.VMEM((2, D, HID), BF),
            pltpu.VMEM((HID, D), BF),
            pltpu.VMEM((2, TOK, D), BF),
            pltpu.VMEM((TOK, D), BF),
            pltpu.VMEM((128, 128), BF),
            pltpu.VMEM((2, TOK, 128), BF),
            pltpu.VMEM((2, 2, TOK, 128), BF),
            pltpu.VMEM((2, TOK, 128), BF),
            pltpu.VMEM((2, 2, TOK, 128), BF),
            pltpu.VMEM((224, 256), BF),
            pltpu.VMEM((256, 224), BF),
            pltpu.VMEM((2, 2, TOK, HALF), BF),
            pltpu.VMEM((2, 2, XROWS, 2 * WIDE), BF),
            pltpu.VMEM((7, 16, 2 * WIDE), BF),
            pltpu.VMEM((2, 7, 16, WIDE), BF),
            pltpu.VMEM((XROWS, HID), BF),
            pltpu.VMEM((224, 256), BF),
            pltpu.VMEM((2, ROWS, 2 * WIDE), BF),
            pltpu.VMEM((2, 2, 4, 64, WIDE), BF),
            pltpu.VMEM((7, 16, 2 * WIDE), BF),
            pltpu.VMEM((2, 7, 16, WIDE), BF),
            pltpu.VMEM((2, 8, 16, 2 * WIDE), BF),
            pltpu.VMEM((2, 2, 8, 16, WIDE), BF),
            pltpu.VMEM((2, TOK, HALF), BF),
            pltpu.VMEM((2, 2, TOK, HALF), BF),
            dma((2,)),
            dma, dma,
            dma, dma((2,)),
            dma, dma((2, 2)),
            dma, dma((2, 8)),
            dma, dma((2, 16)),
            dma, dma((2, 2)),
            dma, dma((2, 8)),
            dma, dma((2,)),
            dma, dma((2, 2)),
            dma, dma((2, 2)),
            dma, dma((2,)),
        ],
        compiler_params=pltpu.CompilerParams(
            collective_id=0, has_side_effects=True, vmem_limit_bytes=60 << 20
        ),
        name="relay",
    )(order, batches, gains, router[0].T, jnp.swapaxes(routes[0], 1, 2), caps, w_in[0], w_down[0])
    return out[None]


def solution(mesh):
    placed = (
        P(None, "expert", None),
        P(),
        P("section", None),
        P("section", None, None),
        P("section", None, "expert", None),
        P("section", None),
        P("section", None, None, "expert"),
        P("section", "expert", None),
    )
    return jax.shard_map(
        local,
        mesh=mesh,
        in_specs=placed,
        out_specs=P("section", None, "expert", None),
        check_vma=False,
    )
```

time: 224 us -> 208 us (0.929)
  Pallas kernels: 217 us -> 206 us
  local copies, waits for them, and re-layouts: 6.27 us -> 2.16 us
    pallas_call x1, Pallas kernels: 217 us -> 206 us  [local(): pl.pallas_call(kernel, out_shape=jax.ShapeDtypeStruct((2, TOK, D), BF), i...]
    unnamed x3 -> x1, local copies, waits for them, and re-layouts: 6.27 us -> 2.16 us
where the time goes in v2:
time: 208 us
  Pallas kernels  206 us (99%)
  local copies, waits for them, and re-layouts  2.16 us (1%)
    pallas_call x1, Pallas kernels, local(): pl.pallas_call(kernel, out_shape=jax.ShapeDtypeStruct((2, TOK, D), BF), i...  206 us

profile of v2, /device:TPU:0, one launch (start us, length us, event | category | flops | bytes accessed | tf_op | source)
XLA Modules:
  0.0 207.7 jit_solution(278234601190414755)
XLA Ops:
  0.0 205.6 %relay.1 = bf16[2,64,3584]{2,1,0:T(8,128)(2,1)} custom-call(s32[4]{0:T(128)} %order_ref.1, bf16[4,64,3584]{2,1,0:T(8,128)(2,1)} %batches_ref.1, f32[1,3584]{1,0:T(1,128)} %gain_ref.1, f32[8,3584]{1,0:T(8,128)} %bitcast.12, s32[2,2,64]{2,1,0:T(2,128)} %bitcast.13, s32[1,8]{1,0:T(1,128)} %caps_ref.1, bf16[2,3584,512]{2,1,0:T(8,128)(2,1)} %bitcast.9, ...), custom_call_target="tpu_custom_call" | custom-call | tf_op jit(solution)/shard_map/relay/pallas_call | solution.py:393
  205.6 2.2 %copy.10 = bf16[1,2,64,3584]{3,2,1,0:T(8,128)(2,1)} copy(bf16[1,2,64,3584]{3,2,1,0:T(8,128)(2,1)} %bitcast.11) | data formatting | bytes 1835008

commit v3 on v2

--- a/solution.py
+++ b/solution.py
@@ -35,8 +35,8 @@
 
 def kernel(
     order_ref, batches_ref, gain_ref, router_ref, routes_ref, caps_ref, w_in_hbm, w_down_hbm, out_ref,
-    w_in, w_down, u_buf, normed, onehot, rk_own, rk_near, gates_own, gates_near, sel, pack,
-    nb, x_buf, sa, sb, hidden, ext_out, out_buf, part, sa2, sn2, ra2, rn2, s3, r3,
+    w_in, w_down, u_buf, normed, onehot, rk_own, rk_near, gates_own, gates_near, pick_main, pick_ext, sel, pack,
+    nb, x_buf, sa, sb, hidden, ext_out, out_buf, part, sa2, sn2, ra2, rn2, s3, r3, total_out,
     w_sem, rk_send, rk_recv, g_send, g_recv, nb_send, nb_recv, a1_send, a1_recv, b_send, b_recv, a2_send, a2_recv,
     part_send, part_recv, ra2_send, ra2_recv, rn2_send, rn2_recv, r3_send, r3_recv, u_send, u_recv,
 ):
@@ -119,24 +119,6 @@
     def layer(step, carry):
         direction = jnp.where(s < 2, step, 1 - step)
 
-        @pl.when(jnp.logical_not(jnp.logical_and(step == 0, outer)))
-        def _():
-            got(u_buf.at[step], u_recv.at[step])
-
-        total = jnp.zeros((TOK, 512), F32)
-        for i in range(D // 512):
-            v = u_buf[step, :, i * 512:(i + 1) * 512].astype(F32)
-            total = total + v * v
-        inv = lax.rsqrt(jnp.sum(total, axis=1, keepdims=True) * (1.0 / D) + 1e-06)
-        for p in range(2):
-            for i in range(p * HALF, (p + 1) * HALF, 256):
-                v = u_buf[step, :, i:i + 256].astype(F32)
-                normed[:, i:i + 256] = (v * inv * gain_ref[:, i:i + 256]).astype(BF)
-            send(
-                normed.at[:, p * HALF:(p + 1) * HALF], nb.at[step, p],
-                nb_send, nb_recv.at[step, p], chip(0, 0, toward[p]),
-            )
-
         def packer(ranks):
             rt = nt(onehot[...], ranks)
             main = (rt == lax.rem(iota((128, TOK), 0), 16).astype(F32)).astype(BF)
@@ -146,8 +128,35 @@
             ext = jnp.logical_and(rt7 == want, lax.rem(rw, 8) == cl // TOK).astype(BF)
             return main, ext
 
-        def packed(tables, source, put):
-            main, ext = tables
+        pick_main[0], pick_ext[0] = packer(rk_own[step])
+
+        @pl.when(step == 0)
+        def _():
+            got(rk_near, rk_recv)
+
+        for p in range(2):
+            pick_main[p + 1], pick_ext[p + 1] = packer(rk_near[p, step])
+
+        @pl.when(jnp.logical_not(jnp.logical_and(step == 0, outer)))
+        def _():
+            got(u_buf.at[step], u_recv.at[step])
+
+        total = jnp.zeros((TOK, 512), F32)
+        for i in range(D // 512):
+            v = u_buf[step, :, i * 512:(i + 1) * 512].astype(F32)
+            total = total + v * v
+        inv = lax.rsqrt(jnp.sum(total, axis=1, keepdims=True) * (1.0 / D) + 1e-06)
+        for p in range(2):
+            for i in range(p * HALF, (p + 1) * HALF, 256):
+                v = u_buf[step, :, i:i + 256].astype(F32)
+                normed[:, i:i + 256] = (v * inv * gain_ref[:, i:i + 256]).astype(BF)
+            send(
+                normed.at[:, p * HALF:(p + 1) * HALF], nb.at[step, p],
+                nb_send, nb_recv.at[step, p], chip(0, 0, toward[p]),
+            )
+
+        def packed(which, source, put):
+            main, ext = pick_main[which], pick_ext[which]
             for i in range(NBLK):
                 put(i * BLK, mm(main, source(i)).astype(BF))
             stack = jnp.concatenate([source(i) for i in range(NBLK)], axis=0)
@@ -185,20 +194,15 @@
                 a2_send, a2_recv.at[step, ch], chip(0, 0, toward[p]),
             )
 
-        tables = packer(rk_own[step])
         for p in range(2):
             def put_own(at, v):
                 x_buf[step, 0, 0:16, p * WIDE + at:p * WIDE + at + BLK] = v[0:16]
                 sa[:, :, p * WIDE + at:p * WIDE + at + BLK] = v[16:128].reshape(7, 16, BLK)
 
-            packed(tables, lambda i: normed[:, p * HALF + i * BLK:p * HALF + (i + 1) * BLK], put_own)
-        for i in (1, 2, 3):
+            packed(0, lambda i: normed[:, p * HALF + i * BLK:p * HALF + (i + 1) * BLK], put_own)
+        for i in range(1, 8):
             send_own(i)
         forward_own(0)
-
-        @pl.when(step == 0)
-        def _():
-            got(rk_near, rk_recv)
 
         for p in range(2):
             def put_near(at, v):
@@ -206,22 +210,16 @@
                 x_buf[step, 0, first:first + 16, p * WIDE + at:p * WIDE + at + BLK] = v[0:16]
                 sb[p, :, :, at:at + BLK] = v[16:128].reshape(7, 16, BLK)
 
-            tables = packer(rk_near[p, step])
             got(nb.at[step, p], nb_recv.at[step, p])
-            packed(tables, lambda i: nb[step, p, :, i * BLK:(i + 1) * BLK], put_near)
+            packed(p + 1, lambda i: nb[step, p, :, i * BLK:(i + 1) * BLK], put_near)
             for i in (1, 2, 3):
                 send_near(p, i)
             forward_near(p, 0)
-        for i in (1, 2, 3):
-            forward_own(i)
-        for i in range(4, 8):
-            send_own(i)
-        for p in range(2):
-            for i in (1, 2, 3):
-                forward_near(p, i)
         for i in range(4, 8):
             for p in range(2):
                 send_near(p, i)
+        for i in range(1, 8):
+            forward_own(i)
 
         router = router_ref[...]
         high = router.astype(BF)
@@ -232,8 +230,10 @@
         for p in range(2):
             send(gates_own.at[step], gates_near.at[step, p], g_send, g_recv.at[step], chip(0, 0, toward[p]))
 
-        for i in range(4, 8):
-            forward_own(i)
+        for group in ((1, 2, 3), (4, 5, 6, 7)):
+            for p in range(2):
+                for i in group:
+                    forward_near(p, i)
 
         @pl.when(step == 0)
         def _():
@@ -258,13 +258,10 @@
             hidden[:, cols] = (jax.nn.silu(g) * v).astype(BF)
 
         def down(ch, p):
-            def tile(n, carry):
-                v = mm(hidden[...], w_down[:, pl.ds(pl.multiple_of(p * HALF + n * BLK, BLK), BLK)]).astype(BF)
-                out_buf[ch, 0:ROWS, pl.ds(pl.multiple_of(p * WIDE + n * BLK, BLK), BLK)] = v[0:ROWS]
-                ext_out[pl.ds(pl.multiple_of(n * 32, 32), 32), :] = v[ROWS:XROWS]
-                return carry
-
-            lax.fori_loop(0, NBLK, tile, 0)
+            for n in range(NBLK):
+                v = mm(hidden[...], w_down[:, p * HALF + n * BLK:p * HALF + (n + 1) * BLK]).astype(BF)
+                out_buf[ch, 0:ROWS, p * WIDE + n * BLK:p * WIDE + (n + 1) * BLK] = v[0:ROWS]
+                ext_out[n * 32:(n + 1) * 32, :] = v[ROWS:XROWS]
             out_buf[ch, 0:ROWS, p * WIDE + HALF:(p + 1) * WIDE] = mm(pack[...], ext_out[...]).astype(BF)
 
         def send_part(ch, p, q):
@@ -289,16 +286,15 @@
                     rn2[step, p, 0] = v
                 elif i:
                     sa2[i - 1, :, lanes(p)] = v
-                    if p:
-                        send(sa2.at[i - 1], ra2.at[step, i], ra2_send, ra2_recv.at[step], chip(dx, -dz, 0))
+                    send(
+                        sa2.at[i - 1, :, lanes(p)], ra2.at[step, i, :, lanes(p)],
+                        ra2_send, ra2_recv.at[step, p], chip(dx, -dz, 0),
+                    )
                 else:
                     ra2[step, 0, :, lanes(p)] = v
 
         arrived(0)
         up(0, 0)
-        for p in range(2):
-            for i in range(4, 8):
-                forward_near(p, i)
         up(0, 1)
         for p in range(2):
             down(0, p)
@@ -348,24 +344,32 @@
             send(s3.at[p], r3.at[step, p], r3_send, r3_recv.at[step, p], chip(0, 0, near[p]))
 
         tables = weights(rk_own[step], gates_own[step])
-        got(ra2.at[step, 1:8], ra2_recv.at[step])
-        for p in range(2):
-            got(r3.at[step, p], r3_recv.at[step, p])
-
-            def put_out(at, v):
+        for p in range(2):
+            got(ra2.at[step, 1:8, :, lanes(p)], ra2_recv.at[step, p])
+
+            def put_sum(at, v):
                 cols = slice(p * HALF + at, p * HALF + at + BLK)
-                v = v + r3[step, p, :, at:at + BLK].astype(F32)
-                out_ref[direction, :, cols] = (u_buf[step, :, cols].astype(F32) + v).astype(BF)
-
-            weighed(tables, lambda at: ra2[step, :, :, p * WIDE + at:p * WIDE + at + BLK].reshape(128, BLK), put_out)
+                total_out[:, cols] = u_buf[step, :, cols].astype(F32) + v
+
+            weighed(tables, lambda at: ra2[step, :, :, p * WIDE + at:p * WIDE + at + BLK].reshape(128, BLK), put_sum)
 
         target = jnp.where(direction == 0, s + 1, s - 1)
         relays = jnp.logical_and(target >= 0, target <= 3)
         target_step = jnp.where(jnp.logical_and(step == 0, outer), 0, 1)
-
-        @pl.when(relays)
-        def _():
-            send(out_ref.at[direction], u_buf.at[target_step], u_send, u_recv.at[target_step], (target, me))
+        for p in range(2):
+            got(r3.at[step, p], r3_recv.at[step, p])
+            half = slice(p * HALF, (p + 1) * HALF)
+            for i in range(NBLK):
+                cols = slice(p * HALF + i * BLK, p * HALF + (i + 1) * BLK)
+                v = total_out[:, cols] + r3[step, p, :, i * BLK:(i + 1) * BLK].astype(F32)
+                out_ref[direction, :, cols] = v.astype(BF)
+
+            @pl.when(relays)
+            def _():
+                send(
+                    out_ref.at[direction, :, half], u_buf.at[target_step, :, half],
+                    u_send, u_recv.at[target_step], (target, me),
+                )
 
         sent(nb.at[step], nb_send)
         sent(sa, a1_send)
@@ -405,6 +409,8 @@
             pltpu.VMEM((2, 2, TOK, 128), BF),
             pltpu.VMEM((2, TOK, 128), BF),
             pltpu.VMEM((2, 2, TOK, 128), BF),
+            pltpu.VMEM((3, 128, TOK), BF),
+            pltpu.VMEM((3, 128, TOK * NBLK), BF),
             pltpu.VMEM((224, 256), BF),
             pltpu.VMEM((256, 224), BF),
             pltpu.VMEM((2, 2, TOK, HALF), BF),
@@ -421,6 +427,7 @@
             pltpu.VMEM((2, 2, 8, 16, WIDE), BF),
             pltpu.VMEM((2, TOK, HALF), BF),
             pltpu.VMEM((2, 2, TOK, HALF), BF),
+            pltpu.VMEM((TOK, D), F32),
             dma((2,)),
             dma, dma,
             dma, dma((2,)),
@@ -429,7 +436,7 @@
             dma, dma((2, 16)),
             dma, dma((2, 2)),
             dma, dma((2, 8)),
-            dma, dma((2,)),
+            dma, dma((2, 2)),
             dma, dma((2, 2)),
             dma, dma((2, 2)),
             dma, dma((2,)),

time: 208 us -> 200 us (0.962)
  Pallas kernels: 206 us -> 198 us
    pallas_call x1, Pallas kernels: 206 us -> 198 us  [local(): pl.pallas_call(kernel, out_shape=jax.ShapeDtypeStruct((2, TOK, D), BF), i...]
where the time goes in v3:
time: 200 us
  Pallas kernels  198 us (99%)
  local copies, waits for them, and re-layouts  2.16 us (1%)
    pallas_call x1, Pallas kernels, local(): pl.pallas_call(kernel, out_shape=jax.ShapeDtypeStruct((2, TOK, D), BF), i...  198 us

profile of v3, /device:TPU:0, one launch (start us, length us, event | category | flops | bytes accessed | tf_op | source)
XLA Modules:
  0.0 200.1 jit_solution(3628245173761859865)
XLA Ops:
  0.0 198.0 %relay.1 = bf16[2,64,3584]{2,1,0:T(8,128)(2,1)} custom-call(s32[4]{0:T(128)} %order_ref.1, bf16[4,64,3584]{2,1,0:T(8,128)(2,1)} %batches_ref.1, f32[1,3584]{1,0:T(1,128)} %gain_ref.1, f32[8,3584]{1,0:T(8,128)} %bitcast.12, s32[2,2,64]{2,1,0:T(2,128)} %bitcast.13, s32[1,8]{1,0:T(1,128)} %caps_ref.1, bf16[2,3584,512]{2,1,0:T(8,128)(2,1)} %bitcast.9, ...), custom_call_target="tpu_custom_call" | custom-call | tf_op jit(solution)/shard_map/relay/pallas_call | solution.py:397
  198.0 2.2 %copy.10 = bf16[1,2,64,3584]{3,2,1,0:T(8,128)(2,1)} copy(bf16[1,2,64,3584]{3,2,1,0:T(8,128)(2,1)} %bitcast.11) | data formatting | bytes 1835008

commit v4 on v3

--- a/solution.py
+++ b/solution.py
@@ -130,12 +130,19 @@
 
         pick_main[0], pick_ext[0] = packer(rk_own[step])
 
-        @pl.when(step == 0)
+        def tables_near(p, carry):
+            pick_main[p + 1], pick_ext[p + 1] = packer(rk_near[p, step])
+            return carry
+
+        first = jnp.logical_and(step == 0, outer)
+
+        @pl.when(jnp.logical_and(step == 0, jnp.logical_not(outer)))
         def _():
             got(rk_near, rk_recv)
 
-        for p in range(2):
-            pick_main[p + 1], pick_ext[p + 1] = packer(rk_near[p, step])
+        @pl.when(jnp.logical_not(first))
+        def _():
+            lax.fori_loop(0, 2, tables_near, 0)
 
         @pl.when(jnp.logical_not(jnp.logical_and(step == 0, outer)))
         def _():
@@ -204,10 +211,24 @@
             send_own(i)
         forward_own(0)
 
+        router = router_ref[...]
+        high = router.astype(BF)
+        low = (router - high.astype(F32)).astype(BF)
+        scores = jax.nn.sigmoid(nt(normed[...], high) + nt(normed[...], low))
+        chosen = jnp.sum(nt(eye, named(step)) * scores, axis=1, keepdims=True)
+        gates_own[step, :, 0:EXPERTS] = (2.5 * scores / chosen).astype(BF)
+        for p in range(2):
+            send(gates_own.at[step], gates_near.at[step, p], g_send, g_recv.at[step], chip(0, 0, toward[p]))
+
+        @pl.when(first)
+        def _():
+            got(rk_near, rk_recv)
+            lax.fori_loop(0, 2, tables_near, 0)
+
         for p in range(2):
             def put_near(at, v):
-                first = near[p] * 64
-                x_buf[step, 0, first:first + 16, p * WIDE + at:p * WIDE + at + BLK] = v[0:16]
+                at_row = near[p] * 64
+                x_buf[step, 0, at_row:at_row + 16, p * WIDE + at:p * WIDE + at + BLK] = v[0:16]
                 sb[p, :, :, at:at + BLK] = v[16:128].reshape(7, 16, BLK)
 
             got(nb.at[step, p], nb_recv.at[step, p])
@@ -221,19 +242,12 @@
         for i in range(1, 8):
             forward_own(i)
 
-        router = router_ref[...]
-        high = router.astype(BF)
-        low = (router - high.astype(F32)).astype(BF)
-        scores = jax.nn.sigmoid(nt(normed[...], high) + nt(normed[...], low))
-        chosen = jnp.sum(nt(eye, named(step)) * scores, axis=1, keepdims=True)
-        gates_own[step, :, 0:EXPERTS] = (2.5 * scores / chosen).astype(BF)
-        for p in range(2):
-            send(gates_own.at[step], gates_near.at[step, p], g_send, g_recv.at[step], chip(0, 0, toward[p]))
-
-        for group in ((1, 2, 3), (4, 5, 6, 7)):
+        for p in range(2):
+            for i in (1, 2, 3):
+                forward_near(p, i)
+        for i in range(4, 8):
             for p in range(2):
-                for i in group:
-                    forward_near(p, i)
+                forward_near(p, i)
 
         @pl.when(step == 0)
         def _():
@@ -303,12 +317,12 @@
         arrived(1)
         up(1, 0)
         up(1, 1)
-        back(0, 0, 1)
         down(1, 0)
         send_part(1, 0, 1)
-        back(0, 1, 1)
         down(1, 1)
         send_part(1, 1, 1)
+        back(0, 0, 1)
+        back(0, 1, 1)
         send_part(1, 0, 0)
         send_part(1, 1, 0)
         back(0, 0, 0)

time: 200 us -> 198 us (0.990)
  Pallas kernels: 198 us -> 195 us
    pallas_call x1, Pallas kernels: 198 us -> 195 us  [local(): pl.pallas_call(kernel, out_shape=jax.ShapeDtypeStruct((2, TOK, D), BF), i...]
where the time goes in v4:
time: 198 us
  Pallas kernels  195 us (98%)
  local copies, waits for them, and re-layouts  2.16 us (1%)
    pallas_call x1, Pallas kernels, local(): pl.pallas_call(kernel, out_shape=jax.ShapeDtypeStruct((2, TOK, D), BF), i...  195 us

profile of v4, /device:TPU:0, one launch (start us, length us, event | category | flops | bytes accessed | tf_op | source)
XLA Modules:
  0.0 197.5 jit_solution(16580887116939742502)
XLA Ops:
  0.0 195.3 %relay.1 = bf16[2,64,3584]{2,1,0:T(8,128)(2,1)} custom-call(s32[4]{0:T(128)} %order_ref.1, bf16[4,64,3584]{2,1,0:T(8,128)(2,1)} %batches_ref.1, f32[1,3584]{1,0:T(1,128)} %gain_ref.1, f32[8,3584]{1,0:T(8,128)} %bitcast.12, s32[2,2,64]{2,1,0:T(2,128)} %bitcast.13, s32[1,8]{1,0:T(1,128)} %caps_ref.1, bf16[2,3584,512]{2,1,0:T(8,128)(2,1)} %bitcast.9, ...), custom_call_target="tpu_custom_call" | custom-call | tf_op jit(solution)/shard_map/relay/pallas_call | solution.py:411
  195.4 2.2 %copy.10 = bf16[1,2,64,3584]{3,2,1,0:T(8,128)(2,1)} copy(bf16[1,2,64,3584]{3,2,1,0:T(8,128)(2,1)} %bitcast.11) | data formatting | bytes 1835008

commit v5 on v4

--- a/solution.py
+++ b/solution.py
@@ -36,7 +36,7 @@
 def kernel(
     order_ref, batches_ref, gain_ref, router_ref, routes_ref, caps_ref, w_in_hbm, w_down_hbm, out_ref,
     w_in, w_down, u_buf, normed, onehot, rk_own, rk_near, gates_own, gates_near, pick_main, pick_ext, sel, pack,
-    nb, x_buf, sa, sb, hidden, ext_out, out_buf, part, sa2, sn2, ra2, rn2, s3, r3, total_out,
+    nb, x_buf, sa, sb, hidden, ext_out, out_buf, part, sa2, sn2, ra2, rn2, s3, r3, total_out, gate_main, gate_ext,
     w_sem, rk_send, rk_recv, g_send, g_recv, nb_send, nb_recv, a1_send, a1_recv, b_send, b_recv, a2_send, a2_recv,
     part_send, part_recv, ra2_send, ra2_recv, rn2_send, rn2_recv, r3_send, r3_recv, u_send, u_recv,
 ):
@@ -307,6 +307,21 @@
                 else:
                     ra2[step, 0, :, lanes(p)] = v
 
+        def weights(ranks, gate):
+            rt, gt = nt(ranks, onehot[...]), nt(gate, onehot[...])
+            main = jnp.where(rt == lax.rem(iota((TOK, 128), 1), 16).astype(F32), gt, 0.0).astype(BF)
+            rw, cl = iota((TOK * NBLK, 128), 0), iota((TOK * NBLK, 128), 1)
+            want = (16 + lax.rem(cl, 16) // 8).astype(F32)
+            take = jnp.logical_and(
+                jnp.concatenate([rt] * NBLK, axis=0) == want, lax.rem(cl, 8) == rw // TOK
+            )
+            return main, jnp.where(take, jnp.concatenate([gt] * NBLK, axis=0), 0.0).astype(BF)
+
+        got(gates_near.at[step], g_recv.at[step])
+        for p in range(2):
+            gate_main[p], gate_ext[p] = weights(rk_near[p, step], gates_near[step, p])
+        gate_main[2], gate_ext[2] = weights(rk_own[step], gates_own[step])
+
         arrived(0)
         up(0, 0)
         up(0, 1)
@@ -331,33 +346,25 @@
             for p in range(2):
                 back(1, p, q)
 
-        def weights(ranks, gate):
-            rt, gt = nt(ranks, onehot[...]), nt(gate, onehot[...])
-            main = jnp.where(rt == lax.rem(iota((TOK, 128), 1), 16).astype(F32), gt, 0.0).astype(BF)
-            rw, cl = iota((TOK * NBLK, 128), 0), iota((TOK * NBLK, 128), 1)
-            want = (16 + lax.rem(cl, 16) // 8).astype(F32)
-            take = jnp.logical_and(
-                jnp.concatenate([rt] * NBLK, axis=0) == want, lax.rem(cl, 8) == rw // TOK
-            )
-            return main, jnp.where(take, jnp.concatenate([gt] * NBLK, axis=0), 0.0).astype(BF)
-
         def weighed(tables, source, put):
             main, ext = tables
             over = mm(ext, source(HALF))
             for i in range(NBLK):
                 put(i * BLK, mm(main, source(i * BLK)) + over[i * TOK:(i + 1) * TOK])
 
-        got(gates_near.at[step], g_recv.at[step])
+        cuts = slice(0, 4 * BLK), slice(4 * BLK, HALF)
+
         for p in range(2):
             def put_back(at, v):
                 s3[p, :, at:at + BLK] = v.astype(BF)
 
-            tables = weights(rk_near[p, step], gates_near[step, p])
+            tables = gate_main[p], gate_ext[p]
             got(rn2.at[step, p, 1:8], rn2_recv.at[step, p])
             weighed(tables, lambda at: rn2[step, p, :, :, at:at + BLK].reshape(128, BLK), put_back)
-            send(s3.at[p], r3.at[step, p], r3_send, r3_recv.at[step, p], chip(0, 0, near[p]))
-
-        tables = weights(rk_own[step], gates_own[step])
+            for h, cut in enumerate(cuts):
+                send(s3.at[p, :, cut], r3.at[step, p, :, cut], r3_send, r3_recv.at[step, p * 2 + h], chip(0, 0, near[p]))
+
+        tables = gate_main[2], gate_ext[2]
         for p in range(2):
             got(ra2.at[step, 1:8, :, lanes(p)], ra2_recv.at[step, p])
 
@@ -370,20 +377,21 @@
         target = jnp.where(direction == 0, s + 1, s - 1)
         relays = jnp.logical_and(target >= 0, target <= 3)
         target_step = jnp.where(jnp.logical_and(step == 0, outer), 0, 1)
-        for p in range(2):
-            got(r3.at[step, p], r3_recv.at[step, p])
-            half = slice(p * HALF, (p + 1) * HALF)
-            for i in range(NBLK):
-                cols = slice(p * HALF + i * BLK, p * HALF + (i + 1) * BLK)
-                v = total_out[:, cols] + r3[step, p, :, i * BLK:(i + 1) * BLK].astype(F32)
-                out_ref[direction, :, cols] = v.astype(BF)
-
-            @pl.when(relays)
-            def _():
-                send(
-                    out_ref.at[direction, :, half], u_buf.at[target_step, :, half],
-                    u_send, u_recv.at[target_step], (target, me),
-                )
+        for h, cut in enumerate(cuts):
+            for p in range(2):
+                got(r3.at[step, p, :, cut], r3_recv.at[step, p * 2 + h])
+                for at in range(cut.start, cut.stop, BLK):
+                    cols = slice(p * HALF + at, p * HALF + at + BLK)
+                    v = total_out[:, cols] + r3[step, p, :, at:at + BLK].astype(F32)
+                    out_ref[direction, :, cols] = v.astype(BF)
+                half = slice(p * HALF + cut.start, p * HALF + cut.stop)
+
+                @pl.when(relays)
+                def _():
+                    send(
+                        out_ref.at[direction, :, half], u_buf.at[target_step, :, half],
+                        u_send, u_recv.at[target_step], (target, me),
+                    )
 
         sent(nb.at[step], nb_send)
         sent(sa, a1_send)
@@ -442,6 +450,8 @@
             pltpu.VMEM((2, TOK, HALF), BF),
             pltpu.VMEM((2, 2, TOK, HALF), BF),
             pltpu.VMEM((TOK, D), F32),
+            pltpu.VMEM((3, TOK, 128), BF),
+            pltpu.VMEM((3, TOK * NBLK, 128), BF),
             dma((2,)),
             dma, dma,
             dma, dma((2,)),
@@ -452,7 +462,7 @@
             dma, dma((2, 8)),
             dma, dma((2, 2)),
             dma, dma((2, 2)),
-            dma, dma((2, 2)),
+            dma, dma((2, 4)),
             dma, dma((2,)),
         ],
         compiler_params=pltpu.CompilerParams(

time: 198 us -> 197 us (level)
  Pallas kernels: 195 us -> 193 us
    pallas_call x1, Pallas kernels: 195 us -> 193 us  [local(): pl.pallas_call(kernel, out_shape=jax.ShapeDtypeStruct((2, TOK, D), BF), i...]
where the time goes in v5:
time: 197 us; the launch traced here: 196 us
  Pallas kernels  193 us (98%)
  local copies, waits for them, and re-layouts  2.16 us (1%)
    pallas_call x1, Pallas kernels, local(): pl.pallas_call(kernel, out_shape=jax.ShapeDtypeStruct((2, TOK, D), BF), i...  193 us

profile of v5, /device:TPU:0, one launch (start us, length us, event | category | flops | bytes accessed | tf_op | source)
XLA Modules:
  0.0 195.5 jit_solution(5456933388172685041)
XLA Ops:
  0.0 193.3 %relay.1 = bf16[2,64,3584]{2,1,0:T(8,128)(2,1)} custom-call(s32[4]{0:T(128)} %order_ref.1, bf16[4,64,3584]{2,1,0:T(8,128)(2,1)} %batches_ref.1, f32[1,3584]{1,0:T(1,128)} %gain_ref.1, f32[8,3584]{1,0:T(8,128)} %bitcast.12, s32[2,2,64]{2,1,0:T(2,128)} %bitcast.13, s32[1,8]{1,0:T(1,128)} %caps_ref.1, bf16[2,3584,512]{2,1,0:T(8,128)(2,1)} %bitcast.9, ...), custom_call_target="tpu_custom_call" | custom-call | tf_op jit(solution)/shard_map/relay/pallas_call | solution.py:419
  193.4 2.2 %copy.10 = bf16[1,2,64,3584]{3,2,1,0:T(8,128)(2,1)} copy(bf16[1,2,64,3584]{3,2,1,0:T(8,128)(2,1)} %bitcast.11) | data formatting | bytes 1835008

commit v6 on v5

--- a/solution.py
+++ b/solution.py
@@ -171,7 +171,11 @@
 
         def send_own(i):
             (dx, dz), ch, j = offs[i], i // 4, i % 4
-            send(sa.at[i - 1], x_buf.at[step, ch, j * 16:j * 16 + 16], a1_send, a1_recv.at[step, i], chip(dx, dz, 0))
+            for p in range(2):
+                send(
+                    sa.at[i - 1, :, lanes(p)], x_buf.at[step, ch, j * 16:j * 16 + 16, lanes(p)],
+                    a1_send, a1_recv.at[step, p * 8 + i], chip(dx, dz, 0),
+                )
 
         def send_near(p, i):
             (dx, dz), ch, at = offs[i], i // 4, near[p] * 64 + i % 4 * 16
@@ -182,10 +186,10 @@
 
         def forward_own(i):
             ch, j = i // 4, i % 4
-            if i:
-                got(x_buf.at[step, ch, j * 16:j * 16 + 16], a1_recv.at[step, i])
             for p in range(2):
                 at = toward[p] * 64 + j * 16
+                if i:
+                    got(x_buf.at[step, ch, j * 16:j * 16 + 16, lanes(p)], a1_recv.at[step, p * 8 + i])
                 send(
                     x_buf.at[step, ch, j * 16:j * 16 + 16, lanes(p)], x_buf.at[step, ch, at:at + 16, lanes(p)],
                     a2_send, a2_recv.at[step, ch], chip(0, 0, near[p]),
@@ -300,10 +304,12 @@
                     rn2[step, p, 0] = v
                 elif i:
                     sa2[i - 1, :, lanes(p)] = v
-                    send(
-                        sa2.at[i - 1, :, lanes(p)], ra2.at[step, i, :, lanes(p)],
-                        ra2_send, ra2_recv.at[step, p], chip(dx, -dz, 0),
-                    )
+                    if ch or p:
+                        cut = lanes(p) if ch else slice(0, 2 * WIDE)
+                        send(
+                            sa2.at[i - 1, :, cut], ra2.at[step, i, :, cut],
+                            ra2_send, ra2_recv.at[step, ch * p], chip(dx, -dz, 0),
+                        )
                 else:
                     ra2[step, 0, :, lanes(p)] = v
 
@@ -365,8 +371,12 @@
                 send(s3.at[p, :, cut], r3.at[step, p, :, cut], r3_send, r3_recv.at[step, p * 2 + h], chip(0, 0, near[p]))
 
         tables = gate_main[2], gate_ext[2]
-        for p in range(2):
-            got(ra2.at[step, 1:8, :, lanes(p)], ra2_recv.at[step, p])
+        rows_first = ra2.at[step, 0:5]
+        for p in range(2):
+            if p == 0:
+                got(rows_first, ra2_recv.at[step, 0])
+            else:
+                got(ra2.at[step, 4:8, :, lanes(1)], ra2_recv.at[step, 1])
 
             def put_sum(at, v):
                 cols = slice(p * HALF + at, p * HALF + at + BLK)
@@ -456,7 +466,7 @@
             dma, dma,
             dma, dma((2,)),
             dma, dma((2, 2)),
-            dma, dma((2, 8)),
+            dma, dma((2, 16)),
             dma, dma((2, 16)),
             dma, dma((2, 2)),
             dma, dma((2, 8)),

time: 197 us -> 196 us (level)
  no operation moved by 1% of the time
where the time goes in v6:
time: 196 us; the launch traced here: 195 us
  Pallas kernels  193 us (98%)
  local copies, waits for them, and re-layouts  2.16 us (1%)
    pallas_call x1, Pallas kernels, local(): pl.pallas_call(kernel, out_shape=jax.ShapeDtypeStruct((2, TOK, D), BF), i...  193 us

profile of v6, /device:TPU:0, one launch (start us, length us, event | category | flops | bytes accessed | tf_op | source)
XLA Modules:
  0.0 195.3 jit_solution(14623092832171079698)
XLA Ops:
  0.0 193.2 %relay.1 = bf16[2,64,3584]{2,1,0:T(8,128)(2,1)} custom-call(s32[4]{0:T(128)} %order_ref.1, bf16[4,64,3584]{2,1,0:T(8,128)(2,1)} %batches_ref.1, f32[1,3584]{1,0:T(1,128)} %gain_ref.1, f32[8,3584]{1,0:T(8,128)} %bitcast.12, s32[2,2,64]{2,1,0:T(2,128)} %bitcast.13, s32[1,8]{1,0:T(1,128)} %caps_ref.1, bf16[2,3584,512]{2,1,0:T(8,128)(2,1)} %bitcast.9, ...), custom_call_target="tpu_custom_call" | custom-call | tf_op jit(solution)/shard_map/relay/pallas_call | solution.py:429
  193.2 2.2 %copy.10 = bf16[1,2,64,3584]{3,2,1,0:T(8,128)(2,1)} copy(bf16[1,2,64,3584]{3,2,1,0:T(8,128)(2,1)} %bitcast.11) | data formatting | bytes 1835008
